TPU v7x, 32 devices: a whole 2x2x4 slice. The times are simulated.
32 devices in a mesh: lon: 8 (over y, x, core), lat: 4 (over z).
Axes of the slice: x: 2, y: 2, z: 4, core: 2. Of those that a mesh axis runs over, the one named last changes fastest.
Arguments:
- control: float32 [2, 16, 256, 1024], P(None, None, 'lat', 'lon'), may hold values from -6 to 6
- land_mask: int32 [256, 1024], P('lat', 'lon'), may hold values 0 or 1
- std_dev: float32 [2, 16], replicated, may hold values from 0.3 to 3
- innovation: float32 [32, 16, 1024], P(None, 'lat', 'lon'), may hold values from -6 to 6
- inverse_var: float32 [32, 16, 1024], P(None, 'lat', 'lon'), may hold values from 0.25 to 4
- obs_row: int32 [16, 1024], P('lat', 'lon'), may hold values from 0 to 62
- obs_col: int32 [16, 1024], P('lat', 'lon'), may hold values from 0 to 126
- frac_row: float32 [16, 1024], P('lat', 'lon'), may hold values from 0 to 1
- frac_col: float32 [16, 1024], P('lat', 'lon'), may hold values from 0 to 1
- counts: int32 [16, 64], P('lat', 'lon'), may hold values from 0 to 16, as said below
Outputs:
- gradient: float32 [2, 16, 256, 1024], P(None, None, 'lat', 'lon')
Inputs may be any that keep to these rules, and one draw needn't show every extreme that they name: `counts`: each tile gets at most 16 live slots from one holder; in every draw some tile gets exactly 16 from every holder. Dense tiles are drawn from the seed.
All inputs are finite; a program needn't handle non-finite values. No bound on the sum of `land_mask` on one device may be relied on, other than what follows from the above.
Results may differ from a plain program's by a relative error of at most 0.000075.
Values sent between devices are 32-bit elements; how exact they have to be, the bound alone decides.
A program may use at most 64 MiB of HBM per device.

v0:
```python
import jax
import jax.numpy as jnp
from jax import lax
from jax.sharding import PartitionSpec as P

HALF = 50


def padded_2(cells, sides, width):
    for axis, dim in sides:
        count = lax.axis_size(axis)
        head = lax.slice_in_dim(cells, 0, width, axis=dim)
        tail = lax.slice_in_dim(cells, cells.shape[dim] - width, cells.shape[dim], axis=dim)
        cells = jnp.concatenate(
            [
                lax.ppermute(tail, axis, [(i, (i + 1) % count) for i in range(count)]),
                cells,
                lax.ppermute(head, axis, [((i + 1) % count, i) for i in range(count)]),
            ],
            axis=dim,
        )
    return cells


def tap_band(n_out, n_in, offset):
    spread = HALF / 2.0
    whole = jnp.arange(-HALF, HALF + 1).astype(jnp.float32)
    norm = jnp.sqrt(jnp.sum(jnp.exp(-(whole / spread) * (whole / spread))))
    out_index = lax.broadcasted_iota(jnp.int32, (n_out, n_in), 0)
    in_index = lax.broadcasted_iota(jnp.int32, (n_out, n_in), 1)
    reach = in_index - out_index - offset
    inside = (reach >= 0) & (reach <= 2 * HALF)
    distance = (reach - HALF).astype(jnp.float32)
    values = jnp.exp(-0.5 * (distance / spread) * (distance / spread)) / norm
    return jnp.where(inside, values, 0.0)


def along_x(field):
    extended = padded_2(field, (("lon", 2),), HALF)
    width = field.shape[2]
    band = tap_band(width, width + 2 * HALF, 0)
    return jnp.einsum("rye,xe->ryx", extended, band, precision=lax.Precision.HIGHEST)


def filter_whole_lines(lines, block):
    count = lines.shape[1] // block
    padded = jnp.pad(lines, ((0, 0), (block, block), (0, 0)))
    blocks = padded.reshape(lines.shape[0], count + 2, block, lines.shape[2])
    band = tap_band(block, 3 * block, block - HALF)
    output = jnp.einsum(
        "ab,rnbc->rnac", band[:, :block], blocks[:, :-2], precision=lax.Precision.HIGHEST
    )
    output = output + jnp.einsum(
        "ab,rnbc->rnac",
        band[:, block : 2 * block],
        blocks[:, 1:-1],
        precision=lax.Precision.HIGHEST,
    )
    output = output + jnp.einsum(
        "ab,rnbc->rnac", band[:, 2 * block :], blocks[:, 2:], precision=lax.Precision.HIGHEST
    )
    return output.reshape(lines.shape)


def along_y(field):
    height = field.shape[1]
    smoothed = filter_whole_lines(
        lax.all_to_all(field, "lat", split_axis=0, concat_axis=1, tiled=True), height
    )
    return lax.all_to_all(smoothed, "lat", split_axis=1, concat_axis=0, tiled=True)


def shards(
    control,
    land_mask,
    std_dev,
    innovation,
    inverse_var,
    obs_row,
    obs_col,
    frac_row,
    frac_col,
    counts,
):
    rows_total = control.shape[0] * control.shape[1]
    tile_rows = control.shape[2]
    tile_cols = control.shape[3]
    fields = control.reshape(rows_total, tile_rows, tile_cols)
    ocean = land_mask.astype(jnp.float32)
    scales = std_dev.reshape(rows_total, 1, 1)
    increment = scales * ocean * along_y(along_x(ocean * fields))
    table = increment.reshape(rows_total, tile_rows * tile_cols)
    corner = obs_row * tile_cols + obs_col
    stencil = [
        (1.0 - frac_row) * (1.0 - frac_col),
        (1.0 - frac_row) * frac_col,
        frac_row * (1.0 - frac_col),
        frac_row * frac_col,
    ]
    shifts = [0, 1, tile_cols, tile_cols + 1]
    columns = jnp.zeros((rows_total,) + corner.shape, jnp.float32)
    for weight, offset in zip(stencil, shifts):
        columns = columns + weight[None] * jnp.take(table, corner + offset, axis=1)
    at_holder = lax.all_to_all(
        lax.all_to_all(columns, "lon", split_axis=2, concat_axis=2, tiled=True),
        "lat",
        split_axis=1,
        concat_axis=1,
        tiled=True,
    )
    weighted_misfit = inverse_var * (at_holder - innovation)
    at_owner = lax.all_to_all(
        lax.all_to_all(weighted_misfit, "lon", split_axis=2, concat_axis=2, tiled=True),
        "lat",
        split_axis=1,
        concat_axis=1,
        tiled=True,
    )
    slot_width = obs_row.shape[1] // counts.shape[1]
    slot_number = lax.broadcasted_iota(jnp.int32, obs_row.shape, 1) % slot_width
    limits = jnp.repeat(counts, slot_width, axis=1)
    live = (slot_number < limits).astype(jnp.float32)
    misfit = at_owner * live[None]
    index_all = jnp.concatenate([(corner + offset).reshape(-1) for offset in shifts])
    values_all = jnp.concatenate(
        [(weight[None] * misfit).reshape(rows_total, -1) for weight in stencil], axis=1
    )
    spread = (
        jnp.zeros((rows_total, tile_rows * tile_cols), jnp.float32).at[:, index_all].add(values_all)
    )
    weighted = spread.reshape(rows_total, tile_rows, tile_cols) * scales
    gradient = fields + ocean * along_x(along_y(ocean * weighted))
    return gradient.reshape(control.shape)


def solution(mesh):
    in_specs = (
        P(None, None, "lat", "lon"),
        P("lat", "lon"),
        P(),
        P(None, "lat", "lon"),
        P(None, "lat", "lon"),
        P("lat", "lon"),
        P("lat", "lon"),
        P("lat", "lon"),
        P("lat", "lon"),
        P("lat", "lon"),
    )
    out_specs = P(None, None, "lat", "lon")
    return jax.shard_map(shards, mesh=mesh, in_specs=in_specs, out_specs=out_specs, check_vma=False)
```

profile of v0, /device:TPU:1, one launch (start us, length us, event | category | flops | bytes accessed | tf_op | source)
XLA Modules:
  0.0 262.2 jit_solution(7240987722631233245)
XLA Ops:
  9.6 12.9 %collective-permute-done = f32[32,64,50]{1,0,2:T(8,128)S(1)} collective-permute-done((f32[32,64,50]{1,0,2:T(8,128)}, f32[32,64,50]{1,0,2:T(8,128)S(1)}, u32[]{:S(2)}, u32[]{:S(2)}) %collective-permute-start) | collective-permute-done | bytes 409632 | tf_op jit(solution)/shard_map/ppermute | solution.py:16
  23.0 3.6 %collective-permute-done.1 = f32[32,64,50]{1,0,2:T(8,128)} collective-permute-done((f32[32,64,50]{1,0,2:T(8,128)}, f32[32,64,50]{1,0,2:T(8,128)}, u32[]{:S(2)}, u32[]{:S(2)}) %collective-permute-start.1) | collective-permute-done | bytes 409632 | tf_op jit(solution)/shard_map/ppermute | solution.py:18
  31.5 4.6 %all-to-all-start = ((f32[32,64,128]{2,1,0:T(8,128)}), f32[32,64,128]{2,1,0:T(8,128)S(1)}, u32[]{:S(2)}, u32[]{:S(2)}) async-start(f32[32,64,128]{2,1,0:T(8,128)} %fusion), calls=%async_computation | async-start | bytes 2097152 | tf_op jit(solution)/shard_map/all_to_all | solution.py:68
  36.1 25.4 %all-to-all-done = f32[32,64,128]{2,1,0:T(8,128)S(1)} async-done(((f32[32,64,128]{2,1,0:T(8,128)}), f32[32,64,128]{2,1,0:T(8,128)S(1)}, u32[]{:S(2)}, u32[]{:S(2)}) %all-to-all-start) | async-done | bytes 1048608 | tf_op jit(solution)/shard_map/all_to_all | solution.py:68
  66.6 3.5 %all-to-all-start.1 = ((f32[8,256,128]{2,0,1:T(8,128)}), f32[8,256,128]{2,0,1:T(8,128)S(1)}, u32[]{:S(2)}, u32[]{:S(2)}) async-start(f32[8,256,128]{2,0,1:T(8,128)} %copy.201), calls=%async_computation.1 | async-start | bytes 2097152 | tf_op jit(solution)/shard_map/all_to_all | solution.py:70
  70.4 25.4 %all-to-all-done.1 = f32[8,256,128]{2,0,1:T(8,128)S(1)} async-done(((f32[8,256,128]{2,0,1:T(8,128)}), f32[8,256,128]{2,0,1:T(8,128)S(1)}, u32[]{:S(2)}, u32[]{:S(2)}) %all-to-all-start.1) | async-done | bytes 1048608 | tf_op jit(solution)/shard_map/all_to_all | solution.py:70
  98.4 4.1 %multiply_multiply_fusion = f32[32,8192]{0,1:T(8,128)} fusion(f32[32,8192]{0,1:T(8,128)} %copy.204, f32[8192]{0:T(1024)S(1)} %get-tuple-element.16, f32[32]{0:T(128)S(1)} %mul.162), kind=kLoop, calls=%fused_computation.5 | loop fusion | flops 524288 | bytes 2130048 | tf_op jit(solution)/shard_map/mul | solution.py:91
  105.8 3.2 %gather_fusion.1 = f32[512,32]{1,0:T(8,128)S(1)} fusion(f32[32,8192]{0,1:T(8,128)} %multiply_multiply_fusion, s32[1024]{0:T(1024)S(1)} %get-tuple-element.34), kind=kCustom, calls=%fused_computation.1.clone | custom fusion | bytes 133120 | tf_op jit(solution)/shard_map/jit(_take)/gather | solution.py:103
  109.2 3.2 %gather_fusion.2 = f32[512,32]{1,0:T(8,128)S(1)} fusion(f32[32,8192]{0,1:T(8,128)} %multiply_multiply_fusion, s32[1024]{0:T(1024)S(1)} %get-tuple-element.33), kind=kCustom, calls=%fused_computation.2.clone | custom fusion | bytes 133120 | tf_op jit(solution)/shard_map/jit(_take)/gather | solution.py:103
  112.5 3.2 %gather_fusion.3 = f32[512,32]{1,0:T(8,128)S(1)} fusion(f32[32,8192]{0,1:T(8,128)} %multiply_multiply_fusion, s32[1024]{0:T(1024)S(1)} %get-tuple-element.32), kind=kCustom, calls=%fused_computation.3.clone | custom fusion | bytes 133120 | tf_op jit(solution)/shard_map/jit(_take)/gather | solution.py:103
  116.9 4.3 %all-to-all-start.2 = ((f32[8,1,2048]{2,1,0:T(1,128)}), f32[8,1,2048]{2,1,0:T(1,128)S(1)}, u32[]{:S(2)}, u32[]{:S(2)}) async-start(f32[8,1,2048]{2,1,0:T(1,128)} %reshape.349), calls=%async_computation.2 | async-start | bytes 131072 | tf_op jit(solution)/shard_map/all_to_all | solution.py:105
  121.4 4.0 %all-to-all-done.2 = f32[8,1,2048]{2,1,0:T(1,128)S(1)} async-done(((f32[8,1,2048]{2,1,0:T(1,128)}), f32[8,1,2048]{2,1,0:T(1,128)S(1)}, u32[]{:S(2)}, u32[]{:S(2)}) %all-to-all-start.2) | async-done | bytes 65568 | tf_op jit(solution)/shard_map/all_to_all | solution.py:105
  127.7 3.3 %all-to-all-start.3 = ((f32[32,4,128]{2,0,1:T(8,128)}), f32[32,4,128]{2,0,1:T(8,128)S(1)}, u32[]{:S(2)}, u32[]{:S(2)}) async-start(f32[32,4,128]{2,0,1:T(8,128)} %copy.214), calls=%async_computation.3 | async-start | bytes 131072 | tf_op jit(solution)/shard_map/all_to_all | solution.py:104
  131.0 4.5 %all-to-all-done.3 = f32[32,4,128]{2,0,1:T(8,128)S(1)} async-done(((f32[32,4,128]{2,0,1:T(8,128)}), f32[32,4,128]{2,0,1:T(8,128)S(1)}, u32[]{:S(2)}, u32[]{:S(2)}) %all-to-all-start.3) | async-done | bytes 65568 | tf_op jit(solution)/shard_map/all_to_all | solution.py:104
  136.6 5.3 %all-to-all-start.4 = ((f32[8,1,2048]{2,1,0:T(1,128)}), f32[8,1,2048]{2,1,0:T(1,128)S(1)}, u32[]{:S(2)}, u32[]{:S(2)}) async-start(f32[8,1,2048]{2,1,0:T(1,128)} %reshape.351), calls=%async_computation.4 | async-start | bytes 131072 | tf_op jit(solution)/shard_map/all_to_all | solution.py:113
  141.8 4.2 %all-to-all-done.4 = f32[8,1,2048]{2,1,0:T(1,128)S(1)} async-done(((f32[8,1,2048]{2,1,0:T(1,128)}), f32[8,1,2048]{2,1,0:T(1,128)S(1)}, u32[]{:S(2)}, u32[]{:S(2)}) %all-to-all-start.4) | async-done | bytes 65568 | tf_op jit(solution)/shard_map/all_to_all | solution.py:113
  147.7 3.3 %all-to-all-start.5 = ((f32[32,4,128]{2,0,1:T(8,128)}), f32[32,4,128]{2,0,1:T(8,128)S(1)}, u32[]{:S(2)}, u32[]{:S(2)}) async-start(f32[32,4,128]{2,0,1:T(8,128)} %copy.218), calls=%async_computation.5 | async-start | bytes 131072 | tf_op jit(solution)/shard_map/all_to_all | solution.py:112
  151.0 4.5 %all-to-all-done.5 = f32[32,4,128]{2,0,1:T(8,128)S(1)} async-done(((f32[32,4,128]{2,0,1:T(8,128)}), f32[32,4,128]{2,0,1:T(8,128)S(1)}, u32[]{:S(2)}, u32[]{:S(2)}) %all-to-all-start.5) | async-done | bytes 65568 | tf_op jit(solution)/shard_map/all_to_all | solution.py:112
  156.0 13.6 %scatter_custom_fusion = f32[32,8192]{0,1:T(8,128)} fusion(s32[2048]{0:T(1024)S(1)} %bitcast.154, f32[2048,32]{1,0:T(8,128)S(1)} %copy.223, f32[]{:T(128)} %constant.23.clone.1), kind=kCustom, calls=%fused_computation.18 | custom fusion | flops 65536 | bytes 1048580 | tf_op jit(solution)/shard_map/scatter-add | solution.py:129
  172.9 27.2 %all_to_all.92 = f32[32,64,128]{2,1,0:T(8,128)S(1)} all-to-all(f32[32,64,128]{2,1,0:T(8,128)S(1)} %multiply_multiply_fusion.1), channel_id=1, replica_groups=mesh['lon'=8,'lat'=4] {'lat'}, dimensions={0} | all-to-all | bytes 2097152 | tf_op jit(solution)/shard_map/all_to_all | solution.py:68
  204.1 27.2 %all_to_all.93 = f32[8,256,128]{2,0,1:T(8,128)S(1)} all-to-all(f32[8,256,128]{2,0,1:T(8,128)S(1)} %copy.226), channel_id=1, replica_groups=mesh['lon'=8,'lat'=4] {'lat'}, dimensions={1} | all-to-all | bytes 2097152 | tf_op jit(solution)/shard_map/all_to_all | solution.py:70
  237.9 13.4 %collective-permute-done.2 = f32[32,64,50]{1,0,2:T(8,128)S(1)} collective-permute-done((f32[32,64,50]{1,0,2:T(8,128)}, f32[32,64,50]{1,0,2:T(8,128)S(1)}, u32[]{:S(2)}, u32[]{:S(2)}) %collective-permute-start.2) | collective-permute-done | bytes 409632 | tf_op jit(solution)/shard_map/ppermute | solution.py:16
  251.9 4.4 %collective-permute-done.3 = f32[32,64,50]{1,0,2:T(8,128)} collective-permute-done((f32[32,64,50]{1,0,2:T(8,128)}, f32[32,64,50]{1,0,2:T(8,128)}, u32[]{:S(2)}, u32[]{:S(2)}) %collective-permute-start.3) | collective-permute-done | bytes 409632 | tf_op jit(solution)/shard_map/ppermute | solution.py:18
  257.9 4.3 %fusion.17 = f32[32,64,128]{2,1,0:T(8,128)} fusion(f32[32,64,128]{2,1,0:T(8,128)} %bitcast.140, f32[32,64,50]{2,1,0:T(8,128)S(1)} %copy.231, f32[32,64,128]{2,1,0:T(8,128)S(1)} %bitcast.131, f32[32,64,50]{2,1,0:T(8,128)S(1)} %copy.230, f32[64,128]{1,0:T(8,128)S(1)} %get-tuple-element.17, f32[]{:T(128)S(6)} %sqrt.2), kind=kOutput, calls=%fused_computation.25 | convolution fusion | flops 719005184 | bytes 3997700 | tf_op jit(solution)/shard_map/rye,xe->ryx/dot_general | solution.py:42
  (89 shorter events, 48.2 us)
Async XLA Ops:
  4.0 18.4 %collective-permute-start = (f32[32,64,50]{1,0,2:T(8,128)}, f32[32,64,50]{1,0,2:T(8,128)S(1)}, u32[]{:S(2)}, u32[]{:S(2)}) collective-permute-start(f32[32,64,50]{1,0,2:T(8,128)} %copy.196), channel_id=1, source_target_pairs={{0,4},{4,8},{8,12},{12,16},{16,20},{20,24},{24,28},{28,0},{1,5},{5... | collective-permute-start | bytes 1228808 | tf_op jit(solution)/shard_map/ppermute | solution.py:16
  8.2 18.5 %collective-permute-start.1 = (f32[32,64,50]{1,0,2:T(8,128)}, f32[32,64,50]{1,0,2:T(8,128)}, u32[]{:S(2)}, u32[]{:S(2)}) collective-permute-start(f32[32,64,50]{1,0,2:T(8,128)} %copy.197), channel_id=1, source_target_pairs={{4,0},{8,4},{12,8},{16,12},{20,16},{24,20},{28,24},{0,28},{5,1},{9... | collective-permute-start | bytes 1228808 | tf_op jit(solution)/shard_map/ppermute | solution.py:18
  31.5 30.1 %all-to-all-start = ((f32[32,64,128]{2,1,0:T(8,128)}), f32[32,64,128]{2,1,0:T(8,128)S(1)}, u32[]{:S(2)}, u32[]{:S(2)}) async-start(f32[32,64,128]{2,1,0:T(8,128)} %fusion), calls=%async_computation | async-start | bytes 2097152 | tf_op jit(solution)/shard_map/all_to_all | solution.py:68
  65.0 5.2 %copy-start.7 = (f32[2,16]{1,0:T(2,128)S(1)}, f32[2,16]{1,0:T(2,128)}, u32[]{:S(2)}) copy-start(f32[2,16]{1,0:T(2,128)} %param.14) | copy-start | bytes 388
  65.0 5.2 %copy-start.3 = (s32[4,128]{1,0:T(4,128)S(1)}, s32[4,128]{1,0:T(4,128)}, u32[]{:S(2)}) copy-start(s32[4,128]{1,0:T(4,128)} %param.18) | copy-start | bytes 6148
  65.0 5.2 %copy-start.4 = (s32[4,128]{1,0:T(4,128)S(1)}, s32[4,128]{1,0:T(4,128)}, u32[]{:S(2)}) copy-start(s32[4,128]{1,0:T(4,128)} %param.17) | copy-start | bytes 6148
  65.0 5.3 %copy-start.5 = (f32[4,128]{1,0:T(4,128)S(1)}, f32[4,128]{1,0:T(4,128)}, u32[]{:S(2)}) copy-start(f32[4,128]{1,0:T(4,128)} %param.20) | copy-start | bytes 6148
  65.0 5.3 %copy-start.6 = (f32[4,128]{1,0:T(4,128)S(1)}, f32[4,128]{1,0:T(4,128)}, u32[]{:S(2)}) copy-start(f32[4,128]{1,0:T(4,128)} %param.19) | copy-start | bytes 6148
  66.6 29.1 %all-to-all-start.1 = ((f32[8,256,128]{2,0,1:T(8,128)}), f32[8,256,128]{2,0,1:T(8,128)S(1)}, u32[]{:S(2)}, u32[]{:S(2)}) async-start(f32[8,256,128]{2,0,1:T(8,128)} %copy.201), calls=%async_computation.1 | async-start | bytes 2097152 | tf_op jit(solution)/shard_map/all_to_all | solution.py:70
  105.7 15.5 %copy-start.2 = (s32[4,8]{1,0:T(4,128)S(1)}, s32[4,8]{1,0:T(4,128)}, u32[]{:S(2)}) copy-start(s32[4,8]{1,0:T(4,128)} %param.21) | copy-start | bytes 388
  109.1 26.5 %copy-start = (f32[32,4,128]{2,1,0:T(4,128)S(1)}, f32[32,4,128]{2,1,0:T(4,128)}, u32[]{:S(2)}) copy-start(f32[32,4,128]{2,1,0:T(4,128)} %param.16) | copy-start | bytes 196612
  109.1 26.5 %copy-start.1 = (f32[32,4,128]{2,1,0:T(4,128)S(1)}, f32[32,4,128]{2,1,0:T(4,128)}, u32[]{:S(2)}) copy-start(f32[32,4,128]{2,1,0:T(4,128)} %param.15) | copy-start | bytes 196612
  116.9 8.5 %all-to-all-start.2 = ((f32[8,1,2048]{2,1,0:T(1,128)}), f32[8,1,2048]{2,1,0:T(1,128)S(1)}, u32[]{:S(2)}, u32[]{:S(2)}) async-start(f32[8,1,2048]{2,1,0:T(1,128)} %reshape.349), calls=%async_computation.2 | async-start | bytes 131072 | tf_op jit(solution)/shard_map/all_to_all | solution.py:105
  127.7 7.9 %all-to-all-start.3 = ((f32[32,4,128]{2,0,1:T(8,128)}), f32[32,4,128]{2,0,1:T(8,128)S(1)}, u32[]{:S(2)}, u32[]{:S(2)}) async-start(f32[32,4,128]{2,0,1:T(8,128)} %copy.214), calls=%async_computation.3 | async-start | bytes 131072 | tf_op jit(solution)/shard_map/all_to_all | solution.py:104
  136.6 9.5 %all-to-all-start.4 = ((f32[8,1,2048]{2,1,0:T(1,128)}), f32[8,1,2048]{2,1,0:T(1,128)S(1)}, u32[]{:S(2)}, u32[]{:S(2)}) async-start(f32[8,1,2048]{2,1,0:T(1,128)} %reshape.351), calls=%async_computation.4 | async-start | bytes 131072 | tf_op jit(solution)/shard_map/all_to_all | solution.py:113
  147.7 7.9 %all-to-all-start.5 = ((f32[32,4,128]{2,0,1:T(8,128)}), f32[32,4,128]{2,0,1:T(8,128)S(1)}, u32[]{:S(2)}, u32[]{:S(2)}) async-start(f32[32,4,128]{2,0,1:T(8,128)} %copy.218), calls=%async_computation.5 | async-start | bytes 131072 | tf_op jit(solution)/shard_map/all_to_all | solution.py:112
  233.6 17.7 %collective-permute-start.2 = (f32[32,64,50]{1,0,2:T(8,128)}, f32[32,64,50]{1,0,2:T(8,128)S(1)}, u32[]{:S(2)}, u32[]{:S(2)}) collective-permute-start(f32[32,64,50]{1,0,2:T(8,128)} %copy.228), channel_id=1, source_target_pairs={{0,4},{4,8},{8,12},{12,16},{16,20},{20,24},{24,28},{28,0},{1,5},{5... | collective-permute-start | bytes 1228808 | tf_op jit(solution)/shard_map/ppermute | solution.py:16
  237.9 18.3 %collective-permute-start.3 = (f32[32,64,50]{1,0,2:T(8,128)}, f32[32,64,50]{1,0,2:T(8,128)}, u32[]{:S(2)}, u32[]{:S(2)}) collective-permute-start(f32[32,64,50]{1,0,2:T(8,128)} %copy.229), channel_id=1, source_target_pairs={{4,0},{8,4},{12,8},{16,12},{20,16},{24,20},{28,24},{0,28},{5,1},{9... | collective-permute-start | bytes 1228808 | tf_op jit(solution)/shard_map/ppermute | solution.py:18
where the time goes:
time: 263 us; the launch traced here: 262 us
  waiting for transfers between devices  102 us (39%)
  blocking collectives  54.5 us (21%)
  local copies, waits for them, and re-layouts  38.3 us (15%)
  starting transfers between devices  29.7 us (11%)
  other arithmetic  22.4 us (9%)
  matrix products  13.8 us (5%)
    all_to_all x1, blocking collectives, along_y(): lax.all_to_all(smoothed, 'lat', split_axis=1, concat_axis=0, tiled=True)  27.2 us
    all_to_all x1, blocking collectives, along_y(): lax.all_to_all(field, 'lat', split_axis=0, concat_axis=1, tiled=True)  27.2 us
    ppermute x2, waiting for transfers between devices, padded_2(): lax.ppermute(tail, axis, [(i, (i + 1) % count) for i in range(count)])  26.2 us
    all_to_all x1, waiting for transfers between devices, along_y(): lax.all_to_all(field, 'lat', split_axis=0, concat_axis=1, tiled=True)  25.4 us
    all_to_all x1, waiting for transfers between devices, along_y(): lax.all_to_all(smoothed, 'lat', split_axis=1, concat_axis=0, tiled=True)  25.4 us
    scatter-add x1, other arithmetic, shards(): jnp.zeros((rows_total, tile_rows * tile_cols), jnp.float32).at[:, index_all]  13.6 us
    gather x8, local copies, waits for them, and re-layouts, shards(): columns = columns + weight[None] * jnp.take(table, corner + offset, axis=1)  13.3 us
    ppermute x2, waiting for transfers between devices, padded_2(): lax.ppermute(head, axis, [((i + 1) % count, i) for i in range(count)])  8.02 us
  transfers between devices with their start and end apart: 10, of which 10 were waited for; matrix products, arithmetic and copies ran while one was open for 2% of the time, Pallas kernels for 0%

commit v1 on v0

--- a/solution.py
+++ b/solution.py
@@ -42,32 +42,24 @@
     return jnp.einsum("rye,xe->ryx", extended, band, precision=lax.Precision.HIGHEST)
 
 
-def filter_whole_lines(lines, block):
-    count = lines.shape[1] // block
-    padded = jnp.pad(lines, ((0, 0), (block, block), (0, 0)))
-    blocks = padded.reshape(lines.shape[0], count + 2, block, lines.shape[2])
-    band = tap_band(block, 3 * block, block - HALF)
-    output = jnp.einsum(
-        "ab,rnbc->rnac", band[:, :block], blocks[:, :-2], precision=lax.Precision.HIGHEST
-    )
-    output = output + jnp.einsum(
-        "ab,rnbc->rnac",
-        band[:, block : 2 * block],
-        blocks[:, 1:-1],
-        precision=lax.Precision.HIGHEST,
-    )
-    output = output + jnp.einsum(
-        "ab,rnbc->rnac", band[:, 2 * block :], blocks[:, 2:], precision=lax.Precision.HIGHEST
-    )
-    return output.reshape(lines.shape)
+def along_y(field):
+    count = lax.axis_size("lat")
+    height = field.shape[1]
+    below = lax.ppermute(field[:, height - HALF :], "lat", [(i, i + 1) for i in range(count - 1)])
+    above = lax.ppermute(field[:, :HALF], "lat", [(i + 1, i) for i in range(count - 1)])
+    extended = jnp.concatenate([below, field, above], axis=1)
+    band = tap_band(height, height + 2 * HALF, 0)
+    return jnp.einsum("ye,rex->ryx", band, extended, precision=lax.Precision.HIGHEST)
 
 
-def along_y(field):
-    height = field.shape[1]
-    smoothed = filter_whole_lines(
-        lax.all_to_all(field, "lat", split_axis=0, concat_axis=1, tiled=True), height
+def to_owner(values):
+    return lax.all_to_all(
+        lax.all_to_all(values, "lon", split_axis=2, concat_axis=2, tiled=True),
+        "lat",
+        split_axis=1,
+        concat_axis=1,
+        tiled=True,
     )
-    return lax.all_to_all(smoothed, "lat", split_axis=1, concat_axis=0, tiled=True)
 
 
 def shards(
@@ -101,21 +93,8 @@
     columns = jnp.zeros((rows_total,) + corner.shape, jnp.float32)
     for weight, offset in zip(stencil, shifts):
         columns = columns + weight[None] * jnp.take(table, corner + offset, axis=1)
-    at_holder = lax.all_to_all(
-        lax.all_to_all(columns, "lon", split_axis=2, concat_axis=2, tiled=True),
-        "lat",
-        split_axis=1,
-        concat_axis=1,
-        tiled=True,
-    )
-    weighted_misfit = inverse_var * (at_holder - innovation)
-    at_owner = lax.all_to_all(
-        lax.all_to_all(weighted_misfit, "lon", split_axis=2, concat_axis=2, tiled=True),
-        "lat",
-        split_axis=1,
-        concat_axis=1,
-        tiled=True,
-    )
+    owned = to_owner(jnp.concatenate([innovation, inverse_var], axis=0))
+    at_owner = owned[rows_total:] * (columns - owned[:rows_total])
     slot_width = obs_row.shape[1] // counts.shape[1]
     slot_number = lax.broadcasted_iota(jnp.int32, obs_row.shape, 1) % slot_width
     limits = jnp.repeat(counts, slot_width, axis=1)

time: 263 us -> 155 us (0.59)
  blocking collectives: 54.5 us -> 0 us
  waiting for transfers between devices: 102 us -> 57.8 us
  starting transfers between devices: 29.7 us -> 24.3 us
  other arithmetic: 22.4 us -> 17.8 us
    all_to_all x6 -> x2, waiting for transfers between devices: 68.1 us -> 0.01 us  [the longest x1 0.01 us: to_owner(): lax.all_to_all(lax.all_to_all(values, 'lon', split_axis=2, concat_axis=2,...]
    all_to_all x2 -> x0, blocking collectives: 54.5 us -> none  [the longest x1 27.2 us: along_y(): lax.all_to_all(smoothed, 'lat', split_axis=1, concat_axis=0, tiled=True)]
    ppermute x0 -> x4, waiting for transfers between devices: none -> 31.2 us  [the longest x2 22.8 us: along_y(): lax.ppermute(field[:, height - HALF:], 'lat', [(i, i + 1) for i in range(...]
    all_to_all x6 -> x2, starting transfers between devices: 24.3 us -> 10.6 us  [the longest x1 6.21 us: to_owner(): lax.all_to_all(lax.all_to_all(values, 'lon', split_axis=2, concat_axis=2,...]
    ppermute x0 -> x4, starting transfers between devices: none -> 9.16 us  [the longest x2 6.37 us: along_y(): lax.ppermute(field[:, height - HALF:], 'lat', [(i, i + 1) for i in range(...]
    ppermute x2, waiting for transfers between devices: 26.2 us -> 20.4 us  [padded_2(): lax.ppermute(tail, axis, [(i, (i + 1) % count) for i in range(count)])]
    mul x2 -> x1, other arithmetic: 5.43 us -> 1.3 us  [shards(): increment = scales * ocean * along_y(along_x(ocean * fields))]
    all_to_all x7 -> x2, local copies, waits for them, and re-layouts: 5.05 us -> 1.32 us  [to_owner(): lax.all_to_all(values, 'lon', split_axis=2, concat_axis=2, tiled=True)]
  transfers between devices with their start and end apart: 10 -> 10, of which waited for: 10 -> 8; matrix products, arithmetic and copies ran while one was open for 2% -> 25% of each run, Pallas kernels for 0% -> 0%
where the time goes in v1:
time: 155 us; the launch traced here: 154 us
  waiting for transfers between devices  57.8 us (37%)
  local copies, waits for them, and re-layouts  40.8 us (26%)
  starting transfers between devices  24.3 us (16%)
  other arithmetic  17.8 us (11%)
  matrix products  12.4 us (8%)
    ppermute x2, waiting for transfers between devices, along_y(): lax.ppermute(field[:, height - HALF:], 'lat', [(i, i + 1) for i in range(...  22.8 us
    ppermute x2, waiting for transfers between devices, padded_2(): lax.ppermute(tail, axis, [(i, (i + 1) % count) for i in range(count)])  20.4 us
    scatter-add x1, other arithmetic, shards(): jnp.zeros((rows_total, tile_rows * tile_cols), jnp.float32).at[:, index_all]  13.6 us
    gather x8, local copies, waits for them, and re-layouts, shards(): columns = columns + weight[None] * jnp.take(table, corner + offset, axis=1)  13.3 us
    ppermute x2, waiting for transfers between devices, along_y(): lax.ppermute(field[:, :HALF], 'lat', [(i + 1, i) for i in range(count - 1)])  8.35 us
    dot_general x2, matrix products, along_x(): jnp.einsum('rye,xe->ryx', extended, band, precision=lax.Precision.HIGHEST)  7.64 us
    ppermute x2, starting transfers between devices, along_y(): lax.ppermute(field[:, height - HALF:], 'lat', [(i, i + 1) for i in range(...  6.37 us
    all_to_all x1, starting transfers between devices, to_owner(): lax.all_to_all(lax.all_to_all(values, 'lon', split_axis=2, concat_axis=2,...  6.21 us
  transfers between devices with their start and end apart: 10, of which 8 were waited for; matrix products, arithmetic and copies ran while one was open for 25% of the time, Pallas kernels for 0%

profile of v1, /device:TPU:1, one launch (start us, length us, event | category | flops | bytes accessed | tf_op | source)
XLA Modules:
  0.0 154.2 jit_solution(91941560659172020)
XLA Ops:
  4.1 2.6 %collective-permute-start = (f32[32,64,50]{1,0,2:T(8,128)}, f32[32,64,50]{1,0,2:T(8,128)}, u32[]{:S(2)}, u32[]{:S(2)}) collective-permute-start(f32[32,64,50]{1,0,2:T(8,128)} %copy.123), channel_id=1, source_target_pairs={{0,4},{4,8},{8,12},{12,16},{16,20},{20,24},{24,28},{28,0},{1,5},{5... | collective-permute-start | bytes 1228808 | tf_op jit(solution)/shard_map/ppermute | solution.py:16
  9.7 4.4 %all-to-all-start = ((f32[8,1,4096]{2,1,0:T(1,128)}), f32[8,1,4096]{2,1,0:T(1,128)S(1)}, u32[]{:S(2)}, u32[]{:S(2)}) async-start(f32[8,1,4096]{2,1,0:T(1,128)} %reshape.332), calls=%async_computation | async-start | bytes 262144 | tf_op jit(solution)/shard_map/all_to_all | solution.py:57
  15.6 6.9 %collective-permute-done = f32[32,64,50]{1,0,2:T(8,128)} collective-permute-done((f32[32,64,50]{1,0,2:T(8,128)}, f32[32,64,50]{1,0,2:T(8,128)}, u32[]{:S(2)}, u32[]{:S(2)}) %collective-permute-start) | collective-permute-done | bytes 409632 | tf_op jit(solution)/shard_map/ppermute | solution.py:16
  24.2 3.3 %collective-permute-done.1 = f32[32,64,50]{1,0,2:T(8,128)} collective-permute-done((f32[32,64,50]{1,0,2:T(8,128)}, f32[32,64,50]{1,0,2:T(8,128)}, u32[]{:S(2)}, u32[]{:S(2)}) %collective-permute-start.1) | collective-permute-done | bytes 409632 | tf_op jit(solution)/shard_map/ppermute | solution.py:18
  27.5 2.6 %copy.126 = f32[32,64,50]{2,1,0:T(8,128)} copy(f32[32,64,50]{1,0,2:T(8,128)} %collective-permute-done.1) | data formatting | bytes 819200 | tf_op jit(solution)/shard_map/ppermute | solution.py:18
  30.2 3.3 %fusion.12 = f32[32,64,128]{2,1,0:T(8,128)S(1)} fusion(f32[32,64,50]{2,1,0:T(8,128)} %copy.126, f32[32,64,128]{2,1,0:T(8,128)S(1)} %bitcast_multiply_fusion, f32[32,64,50]{2,1,0:T(8,128)S(1)} %copy.125, f32[]{:T(128)S(6)} %sqrt.2), kind=kOutput, calls=%fused_computation.17 | convolution fusion | flops 718480896 | bytes 2916356 | tf_op jit(solution)/shard_map/rye,xe->ryx/dot_general | solution.py:42
  33.8 3.2 %collective-permute-start.2 = (f32[32,50,128]{2,0,1:T(8,128)S(1)}, f32[32,50,128]{2,0,1:T(8,128)S(1)}, u32[]{:S(2)}, u32[]{:S(2)}) collective-permute-start(f32[32,50,128]{2,0,1:T(8,128)S(1)} %copy.127), channel_id=1, source_target_pairs={{0,1},{1,2},{2,3},{4,5},{5,6},{6,7},{8,9},{9,10},{10,11},{12,13},{... | collective-permute-start | bytes 2457608 | tf_op jit(solution)/shard_map/ppermute | solution.py:48
  42.0 6.2 %all-to-all-start.1 = ((f32[64,4,128]{2,0,1:T(8,128)}), f32[64,4,128]{2,0,1:T(8,128)S(1)}, u32[]{:S(2)}, u32[]{:S(2)}) async-start(f32[64,4,128]{2,0,1:T(8,128)} %copy.122), calls=%async_computation.1 | async-start | bytes 262144 | tf_op jit(solution)/shard_map/all_to_all | solution.py:56
  48.2 6.8 %collective-permute-done.2 = f32[32,50,128]{2,0,1:T(8,128)S(1)} collective-permute-done((f32[32,50,128]{2,0,1:T(8,128)S(1)}, f32[32,50,128]{2,0,1:T(8,128)S(1)}, u32[]{:S(2)}, u32[]{:S(2)}) %collective-permute-start.2) | collective-permute-done | bytes 819232 | tf_op jit(solution)/shard_map/ppermute | solution.py:48
  55.5 4.7 %collective-permute-done.3 = f32[32,50,128]{2,0,1:T(8,128)} collective-permute-done((f32[32,50,128]{2,0,1:T(8,128)}, f32[32,50,128]{2,0,1:T(8,128)}, u32[]{:S(2)}, u32[]{:S(2)}) %collective-permute-start.3) | collective-permute-done | bytes 819232 | tf_op jit(solution)/shard_map/ppermute | solution.py:49
  61.8 2.4 %fusion.38 = f32[32,64,128]{2,1,0:T(8,128)S(1)} fusion(f32[32,50,128]{2,1,0:T(8,128)S(1)} %copy.130, f32[32,64,128]{2,1,0:T(8,128)S(1)} %fusion.12, f32[32,50,128]{2,1,0:T(8,128)S(1)} %copy.129, f32[32]{0:T(128)S(1)} %mul.76, f32[64,128]{1,0:T(8,128)S(1)} %convert_element_type.24, f32[]{:T(128)S(6)} %sqrt.2), kind=kOutput, calls=%fused_computation.35 | convolution fusion | flops 517882624 | bytes 3768452 | tf_op jit(solution)/shard_map/ye,rex->ryx/dot_general | solution.py:52
  64.2 2.7 %copy.154 = f32[32,64,128]{0,2,1:T(8,128)} copy(f32[32,64,128]{2,1,0:T(8,128)S(1)} %fusion.38) | data formatting | bytes 2097152 | tf_op jit(solution)/shard_map/reshape | solution.py:84
  66.9 3.2 %gather_fusion = f32[512,32]{1,0:T(8,128)S(1)} fusion(f32[32,8192]{0,1:T(8,128)} %bitcast.90, s32[1024]{0:T(1024)S(1)} %get-tuple-element.38), kind=kCustom, calls=%fused_computation.clone | custom fusion | bytes 133120 | tf_op jit(solution)/shard_map/jit(_take)/gather | solution.py:95
  70.2 3.2 %gather_fusion.1 = f32[512,32]{1,0:T(8,128)S(1)} fusion(f32[32,8192]{0,1:T(8,128)} %bitcast.91, s32[1024]{0:T(1024)S(1)} %get-tuple-element.37), kind=kCustom, calls=%fused_computation.1.clone | custom fusion | bytes 133120 | tf_op jit(solution)/shard_map/jit(_take)/gather | solution.py:95
  73.5 3.2 %gather_fusion.2 = f32[512,32]{1,0:T(8,128)S(1)} fusion(f32[32,8192]{0,1:T(8,128)} %bitcast.92, s32[1024]{0:T(1024)S(1)} %get-tuple-element.36), kind=kCustom, calls=%fused_computation.2.clone | custom fusion | bytes 133120 | tf_op jit(solution)/shard_map/jit(_take)/gather | solution.py:95
  76.8 3.2 %gather_fusion.3 = f32[512,32]{1,0:T(8,128)S(1)} fusion(f32[32,8192]{0,1:T(8,128)} %bitcast.93, s32[1024]{0:T(1024)S(1)} %get-tuple-element.35), kind=kCustom, calls=%fused_computation.3.clone | custom fusion | bytes 133120 | tf_op jit(solution)/shard_map/jit(_take)/gather | solution.py:95
  80.7 13.6 %scatter_custom_fusion = f32[32,8192]{0,1:T(8,128)} fusion(s32[2048]{0:T(1024)S(1)} %bitcast.105, f32[2048,32]{1,0:T(8,128)S(1)} %copy.143, f32[]{:T(128)} %constant.21.clone.1), kind=kCustom, calls=%fused_computation.29 | custom fusion | flops 65536 | bytes 1048580 | tf_op jit(solution)/shard_map/scatter-add | solution.py:108
  94.3 3.0 %copy.153 = f32[32,64,128]{2,1,0:T(8,128)S(1)} copy(f32[32,64,128]{0,2,1:T(8,128)} %bitcast.89) | data formatting | bytes 2097152 | tf_op jit(solution)/shard_map/reshape | solution.py:110
  97.8 3.2 %collective-permute-start.4 = (f32[32,50,128]{2,0,1:T(8,128)S(1)}, f32[32,50,128]{2,0,1:T(8,128)S(1)}, u32[]{:S(2)}, u32[]{:S(2)}) collective-permute-start(f32[32,50,128]{2,0,1:T(8,128)S(1)} %copy.145), channel_id=1, source_target_pairs={{0,1},{1,2},{2,3},{4,5},{5,6},{6,7},{8,9},{9,10},{10,11},{12,13},{... | collective-permute-start | bytes 2457608 | tf_op jit(solution)/shard_map/ppermute | solution.py:48
  102.7 16.0 %collective-permute-done.4 = f32[32,50,128]{2,0,1:T(8,128)S(1)} collective-permute-done((f32[32,50,128]{2,0,1:T(8,128)S(1)}, f32[32,50,128]{2,0,1:T(8,128)S(1)}, u32[]{:S(2)}, u32[]{:S(2)}) %collective-permute-start.4) | collective-permute-done | bytes 819232 | tf_op jit(solution)/shard_map/ppermute | solution.py:48
  119.3 3.7 %collective-permute-done.5 = f32[32,50,128]{2,0,1:T(8,128)S(1)} collective-permute-done((f32[32,50,128]{2,0,1:T(8,128)S(1)}, f32[32,50,128]{2,0,1:T(8,128)S(1)}, u32[]{:S(2)}, u32[]{:S(2)}) %collective-permute-start.5) | collective-permute-done | bytes 819232 | tf_op jit(solution)/shard_map/ppermute | solution.py:49
  131.3 13.5 %collective-permute-done.6 = f32[32,64,50]{1,0,2:T(8,128)S(1)} collective-permute-done((f32[32,64,50]{1,0,2:T(8,128)}, f32[32,64,50]{1,0,2:T(8,128)S(1)}, u32[]{:S(2)}, u32[]{:S(2)}) %collective-permute-start.6) | collective-permute-done | bytes 409632 | tf_op jit(solution)/shard_map/ppermute | solution.py:16
  145.3 2.8 %collective-permute-done.7 = f32[32,64,50]{1,0,2:T(8,128)} collective-permute-done((f32[32,64,50]{1,0,2:T(8,128)}, f32[32,64,50]{1,0,2:T(8,128)}, u32[]{:S(2)}, u32[]{:S(2)}) %collective-permute-start.7) | collective-permute-done | bytes 409632 | tf_op jit(solution)/shard_map/ppermute | solution.py:18
  149.9 4.3 %fusion.29 = f32[32,64,128]{2,1,0:T(8,128)} fusion(f32[32,64,128]{2,1,0:T(8,128)} %bitcast.94, f32[32,64,50]{2,1,0:T(8,128)S(1)} %copy.152, f32[32,64,128]{2,1,0:T(8,128)S(1)} %fusion.32, f32[32,64,50]{2,1,0:T(8,128)S(1)} %copy.151, f32[64,128]{1,0:T(8,128)S(1)} %convert_element_type.24, f32[]{:T(128)S(6)} %sqrt.2), kind=kOutput, calls=%fused_computation.32 | convolution fusion | flops 719005184 | bytes 3997700 | tf_op jit(solution)/shard_map/rye,xe->ryx/dot_general | solution.py:42
  (80 shorter events, 30.8 us)
Async XLA Ops:
  2.4 5.8 %copy-start = (f32[32,4,128]{2,1,0:T(4,128)S(1)}, f32[32,4,128]{2,1,0:T(4,128)}, u32[]{:S(2)}) copy-start(f32[32,4,128]{2,1,0:T(4,128)} %param.15) | copy-start | bytes 196612
  2.5 6.0 %copy-start.1 = (f32[32,4,128]{2,1,0:T(4,128)S(1)}, f32[32,4,128]{2,1,0:T(4,128)}, u32[]{:S(2)}) copy-start(f32[32,4,128]{2,1,0:T(4,128)} %param.16) | copy-start | bytes 196612
  2.5 12.9 %copy-start.2 = (s32[4,8]{1,0:T(4,128)S(1)}, s32[4,8]{1,0:T(4,128)}, u32[]{:S(2)}) copy-start(s32[4,8]{1,0:T(4,128)} %param.21) | copy-start | bytes 388
  2.5 13.0 %copy-start.3 = (s32[4,128]{1,0:T(4,128)S(1)}, s32[4,128]{1,0:T(4,128)}, u32[]{:S(2)}) copy-start(s32[4,128]{1,0:T(4,128)} %param.18) | copy-start | bytes 6148
  2.5 13.0 %copy-start.4 = (s32[4,128]{1,0:T(4,128)S(1)}, s32[4,128]{1,0:T(4,128)}, u32[]{:S(2)}) copy-start(s32[4,128]{1,0:T(4,128)} %param.17) | copy-start | bytes 6148
  4.1 18.4 %collective-permute-start = (f32[32,64,50]{1,0,2:T(8,128)}, f32[32,64,50]{1,0,2:T(8,128)}, u32[]{:S(2)}, u32[]{:S(2)}) collective-permute-start(f32[32,64,50]{1,0,2:T(8,128)} %copy.123), channel_id=1, source_target_pairs={{0,4},{4,8},{8,12},{12,16},{16,20},{20,24},{24,28},{28,0},{1,5},{5... | collective-permute-start | bytes 1228808 | tf_op jit(solution)/shard_map/ppermute | solution.py:16
  8.2 19.3 %collective-permute-start.1 = (f32[32,64,50]{1,0,2:T(8,128)}, f32[32,64,50]{1,0,2:T(8,128)}, u32[]{:S(2)}, u32[]{:S(2)}) collective-permute-start(f32[32,64,50]{1,0,2:T(8,128)} %copy.124), channel_id=1, source_target_pairs={{4,0},{8,4},{12,8},{16,12},{20,16},{24,20},{28,24},{0,28},{5,1},{9... | collective-permute-start | bytes 1228808 | tf_op jit(solution)/shard_map/ppermute | solution.py:18
  9.7 29.9 %all-to-all-start = ((f32[8,1,4096]{2,1,0:T(1,128)}), f32[8,1,4096]{2,1,0:T(1,128)S(1)}, u32[]{:S(2)}, u32[]{:S(2)}) async-start(f32[8,1,4096]{2,1,0:T(1,128)} %reshape.332), calls=%async_computation | async-start | bytes 262144 | tf_op jit(solution)/shard_map/all_to_all | solution.py:57
  33.5 5.9 %copy-start.5 = (f32[4,128]{1,0:T(4,128)S(1)}, f32[4,128]{1,0:T(4,128)}, u32[]{:S(2)}) copy-start(f32[4,128]{1,0:T(4,128)} %param.20) | copy-start | bytes 6148
  33.5 5.9 %copy-start.6 = (f32[4,128]{1,0:T(4,128)S(1)}, f32[4,128]{1,0:T(4,128)}, u32[]{:S(2)}) copy-start(f32[4,128]{1,0:T(4,128)} %param.19) | copy-start | bytes 6148
  33.5 5.9 %copy-start.7 = (f32[2,16]{1,0:T(2,128)S(1)}, f32[2,16]{1,0:T(2,128)}, u32[]{:S(2)}) copy-start(f32[2,16]{1,0:T(2,128)} %param.14) | copy-start | bytes 388
  33.8 21.1 %collective-permute-start.2 = (f32[32,50,128]{2,0,1:T(8,128)S(1)}, f32[32,50,128]{2,0,1:T(8,128)S(1)}, u32[]{:S(2)}, u32[]{:S(2)}) collective-permute-start(f32[32,50,128]{2,0,1:T(8,128)S(1)} %copy.127), channel_id=1, source_target_pairs={{0,1},{1,2},{2,3},{4,5},{5,6},{6,7},{8,9},{9,10},{10,11},{12,13},{... | collective-permute-start | bytes 2457608 | tf_op jit(solution)/shard_map/ppermute | solution.py:48
  38.1 22.1 %collective-permute-start.3 = (f32[32,50,128]{2,0,1:T(8,128)}, f32[32,50,128]{2,0,1:T(8,128)}, u32[]{:S(2)}, u32[]{:S(2)}) collective-permute-start(f32[32,50,128]{2,0,1:T(8,128)} %copy.128), channel_id=1, source_target_pairs={{1,0},{2,1},{3,2},{5,4},{6,5},{7,6},{9,8},{10,9},{11,10},{13,12},{... | collective-permute-start | bytes 2457608 | tf_op jit(solution)/shard_map/ppermute | solution.py:49
  42.0 38.2 %all-to-all-start.1 = ((f32[64,4,128]{2,0,1:T(8,128)}), f32[64,4,128]{2,0,1:T(8,128)S(1)}, u32[]{:S(2)}, u32[]{:S(2)}) async-start(f32[64,4,128]{2,0,1:T(8,128)} %copy.122), calls=%async_computation.1 | async-start | bytes 262144 | tf_op jit(solution)/shard_map/all_to_all | solution.py:56
  97.8 20.9 %collective-permute-start.4 = (f32[32,50,128]{2,0,1:T(8,128)S(1)}, f32[32,50,128]{2,0,1:T(8,128)S(1)}, u32[]{:S(2)}, u32[]{:S(2)}) collective-permute-start(f32[32,50,128]{2,0,1:T(8,128)S(1)} %copy.145), channel_id=1, source_target_pairs={{0,1},{1,2},{2,3},{4,5},{5,6},{6,7},{8,9},{9,10},{10,11},{12,13},{... | collective-permute-start | bytes 2457608 | tf_op jit(solution)/shard_map/ppermute | solution.py:48
  101.2 21.7 %collective-permute-start.5 = (f32[32,50,128]{2,0,1:T(8,128)S(1)}, f32[32,50,128]{2,0,1:T(8,128)S(1)}, u32[]{:S(2)}, u32[]{:S(2)}) collective-permute-start(f32[32,50,128]{2,0,1:T(8,128)S(1)} %copy.146), channel_id=1, source_target_pairs={{1,0},{2,1},{3,2},{5,4},{6,5},{7,6},{9,8},{10,9},{11,10},{13,12},{... | collective-permute-start | bytes 2457608 | tf_op jit(solution)/shard_map/ppermute | solution.py:49
  127.7 17.0 %collective-permute-start.6 = (f32[32,64,50]{1,0,2:T(8,128)}, f32[32,64,50]{1,0,2:T(8,128)S(1)}, u32[]{:S(2)}, u32[]{:S(2)}) collective-permute-start(f32[32,64,50]{1,0,2:T(8,128)} %copy.149), channel_id=1, source_target_pairs={{0,4},{4,8},{8,12},{12,16},{16,20},{20,24},{24,28},{28,0},{1,5},{5... | collective-permute-start | bytes 1228808 | tf_op jit(solution)/shard_map/ppermute | solution.py:16
  131.2 16.9 %collective-permute-start.7 = (f32[32,64,50]{1,0,2:T(8,128)}, f32[32,64,50]{1,0,2:T(8,128)}, u32[]{:S(2)}, u32[]{:S(2)}) collective-permute-start(f32[32,64,50]{1,0,2:T(8,128)} %copy.150), channel_id=1, source_target_pairs={{4,0},{8,4},{12,8},{16,12},{20,16},{24,20},{28,24},{0,28},{5,1},{9... | collective-permute-start | bytes 1228808 | tf_op jit(solution)/shard_map/ppermute | solution.py:18

commit v2 on v1

v2 whole, which is shorter than its diff:
```python
import functools

import jax
import jax.numpy as jnp
import numpy as np
from jax import lax
from jax.experimental import pallas as pl
from jax.experimental.pallas import tpu as pltpu
from jax.sharding import PartitionSpec as P

HALF = 50
SPREAD = HALF / 2.0
_TAPS = np.exp(-0.5 * (np.arange(-HALF, HALF + 1) / SPREAD) ** 2)
NORM = float(1.0 / np.sqrt(np.sum(_TAPS * _TAPS)))
CHUNK = 512
GROUP = 8
VMEM_LIMIT = 48 * 1024 * 1024
VMEM = pl.BlockSpec(memory_space=pltpu.VMEM)


def split(x):
    hi = x.astype(jnp.bfloat16)
    lo = (x - hi.astype(jnp.float32)).astype(jnp.bfloat16)
    return hi, lo


def taps(distance):
    values = jnp.exp(distance * distance * (-0.5 / (SPREAD * SPREAD))) * NORM
    return jnp.where(jnp.abs(distance) < HALF + 0.5, values, 0.0)


def iota(shape, dim):
    return lax.broadcasted_iota(jnp.int32, shape, dim).astype(jnp.float32)


def meta_kernel(mask_ref, row_ref, col_ref, frow_ref, fcol_ref, counts_ref, out_ref):
    mask = mask_ref[...].astype(jnp.bfloat16)
    height, width = mask.shape
    holders, lanes = row_ref.shape
    tiles = counts_ref.shape[1]
    cap = lanes // tiles
    tile = lax.broadcasted_iota(jnp.int32, (tiles, lanes), 0)
    lane = lax.broadcasted_iota(jnp.int32, (tiles, lanes), 1)
    inside = (lane >= tile * cap) & (lane < tile * cap + cap)
    repeat = jnp.where(inside, 1.0, 0.0).astype(jnp.bfloat16)
    first = jnp.sum(jnp.where(inside, tile * cap, 0).astype(jnp.float32), axis=0, keepdims=True)
    number = iota((1, lanes), 1) - first
    limits = jnp.dot(
        counts_ref[...].astype(jnp.float32).astype(jnp.bfloat16),
        repeat,
        preferred_element_type=jnp.float32,
    )
    for s in range(holders):
        row = row_ref[pl.ds(s, 1), :].astype(jnp.float32)
        col = col_ref[pl.ds(s, 1), :].astype(jnp.float32)
        a = frow_ref[pl.ds(s, 1), :]
        b = fcol_ref[pl.ds(s, 1), :]
        x = iota((width, lanes), 0) - col
        at_left = jnp.where(x == 0.0, 1.0, 0.0).astype(jnp.bfloat16)
        at_right = jnp.where(x == 1.0, 1.0, 0.0).astype(jnp.bfloat16)
        left = jnp.dot(mask, at_left, preferred_element_type=jnp.float32)
        right = jnp.dot(mask, at_right, preferred_element_type=jnp.float32)
        y = iota((height, lanes), 0) - row
        m00 = jnp.sum(jnp.where(y == 0.0, left, 0.0), axis=0, keepdims=True)
        m01 = jnp.sum(jnp.where(y == 0.0, right, 0.0), axis=0, keepdims=True)
        m10 = jnp.sum(jnp.where(y == 1.0, left, 0.0), axis=0, keepdims=True)
        m11 = jnp.sum(jnp.where(y == 1.0, right, 0.0), axis=0, keepdims=True)
        live = jnp.where(number < limits[s : s + 1], 1.0, 0.0)
        at = pl.ds(s * lanes, lanes)
        out_ref[0:1, at] = row
        out_ref[1:2, at] = col
        out_ref[2:3, at] = (1.0 - a) * (1.0 - b) * m00
        out_ref[3:4, at] = (1.0 - a) * b * m01
        out_ref[4:5, at] = a * (1.0 - b) * m10
        out_ref[5:6, at] = a * b * m11
        out_ref[6:7, at] = live
        out_ref[7:8, at] = live


def neighbours(n_lon, n_lat):
    lon, lat = lax.axis_index("lon"), lax.axis_index("lat")
    found = []
    for t in range(9):
        if t == 4:
            continue
        dp, dq = t // 3 - 1, t % 3 - 1
        there = (lat + dp >= 0) & (lat + dp < n_lat)
        target = {"lon": lax.rem(lon + dq + n_lon, n_lon), "lat": lat + dp}
        found.append((t, there, target, dp))
    return found


def guarded(dp, there, body):
    if dp == 0:
        body()
    else:
        pl.when(there)(body)


def greet(near):
    barrier = pltpu.get_barrier_semaphore()
    for _, there, target, dp in near:
        guarded(dp, there, lambda target=target: pl.semaphore_signal(barrier, inc=1, device_id=target))
    peers = sum(jnp.where(there, 1, 0) for _, there, _, _ in near)
    pl.semaphore_wait(barrier, peers)


def exchange(near, source, target_ref, send_sem, recv_sem):
    copies = []
    for t, there, target, dp in near:
        copy = pltpu.make_async_remote_copy(
            src_ref=source(t),
            dst_ref=target_ref.at[8 - t],
            send_sem=send_sem.at[t],
            recv_sem=recv_sem.at[8 - t],
            device_id=target,
        )
        guarded(dp, there, copy.start)
        copies.append((t, there, dp, copy))
    return copies


def finish(near, copies, target_ref, recv_sem):
    for t, there, dp, copy in copies:
        guarded(dp, there, copy.wait_send)
    for t, there, target, dp in near:
        arrival = pltpu.make_async_remote_copy(
            src_ref=target_ref.at[t],
            dst_ref=target_ref.at[t],
            send_sem=recv_sem.at[t],
            recv_sem=recv_sem.at[t],
            device_id=target,
        )
        guarded(dp, there, arrival.wait_recv)


def clear_missing(near, ref):
    for t, there, _, dp in near:
        if dp == 0:
            continue

        @pl.when(jnp.logical_not(there))
        def _():
            ref[t] = jnp.zeros(ref.shape[1:], ref.dtype)


def share_kernel(n_lon, n_lat, meta_ref, out_ref, send_sem, recv_sem):
    near = neighbours(n_lon, n_lat)
    greet(near)
    copies = exchange(near, lambda t: meta_ref, out_ref, send_sem, recv_sem)
    out_ref[4] = meta_ref[...]
    clear_missing(near, out_ref)
    finish(near, copies, out_ref, recv_sem)


def misfit_kernel(
    n_lon, n_lat, part_ref, owned_ref, meta_ref, std_ref, out_ref,
    landed, mine, send_sem, recv_sem, send_sem_2, recv_sem_2,
):
    near = neighbours(n_lon, n_lat)
    greet(near)
    copies = exchange(near, lambda t: part_ref.at[t], landed, send_sem, recv_sem)
    clear_missing(near, landed)
    clear_missing(near, out_ref)
    finish(near, copies, landed, recv_sem)
    total = part_ref[4]
    for t in range(9):
        if t != 4:
            total = total + landed[t]
    rows = total.shape[0]
    scale = std_ref[...]
    live = meta_ref[6:7, :]
    mine[...] = scale * owned_ref[rows:, :] * (scale * total - owned_ref[:rows, :]) * live
    out_ref[4] = mine[...]
    copies = exchange(near, lambda t: mine, out_ref, send_sem_2, recv_sem_2)
    finish(near, copies, out_ref, recv_sem_2)


def tables(meta, t, height, width):
    dp = (t // 3 - 1).astype(jnp.float32) * height
    dq = (t % 3 - 1).astype(jnp.float32) * width
    chunk = meta.shape[1]
    y = meta[0:1] + dp - iota((height, chunk), 0)
    x = meta[1:2] + dq - iota((width, chunk), 0)
    along_y = [taps(y), taps(y + 1.0)]
    left, right = taps(x), taps(x + 1.0)
    along_x = [
        meta[2:3] * left + meta[3:4] * right,
        meta[4:5] * left + meta[5:6] * right,
    ]
    return along_y, along_x


def forward_kernel(meta_ref, control_ref, mask_ref, out_ref, lhs, ys, xs):
    t = pl.program_id(0)
    levels, height, width = control_ref.shape

    @pl.when((t == 0) & (pl.program_id(1) == 0))
    def _():
        mask = mask_ref[...].astype(jnp.float32)

        @pl.loop(0, levels)
        def _(l):
            hi, lo = split(control_ref[l] * mask)
            at = pl.ds(pl.multiple_of(l * height, height), height)
            lhs[at, 0:width] = hi
            lhs[at, width : 2 * width] = hi
            lhs[at, 2 * width : 3 * width] = lo

    along_y, along_x = tables(meta_ref[0], t, height, width)
    for i in range(2):
        ys[i] = along_y[i]
        hi, lo = split(along_x[i])
        xs[i, 0:width] = hi
        xs[i, width : 2 * width] = lo
        xs[i, 2 * width : 3 * width] = hi

    rows = GROUP * height

    @pl.loop(0, levels // GROUP)
    def _(g):
        left = lhs[pl.ds(pl.multiple_of(g * rows, rows), rows), :]
        total = None
        for i in range(2):
            wide = jnp.dot(left, xs[i], preferred_element_type=jnp.float32)
            term = jnp.sum(wide.reshape(GROUP, height, -1) * ys[i][None], axis=1)
            total = term if total is None else total + term
        out_ref[0, pl.ds(pl.multiple_of(g * GROUP, GROUP), GROUP), :] = total


def backward_kernel(meta_ref, v_ref, control_ref, mask_ref, out_ref, ys, xs):
    t, c = pl.program_id(0), pl.program_id(1)
    levels, height, width = control_ref.shape

    @pl.when((t == 0) & (c == 0))
    def _():
        out_ref[...] = jnp.zeros_like(out_ref)

    along_y, along_x = tables(meta_ref[0], t, height, width)
    chunk = along_x[0].shape[1]
    for i in range(2):
        ys[i] = along_y[i]
        hi, lo = split(along_x[i])
        xs[0:width, i * chunk : (i + 1) * chunk] = hi
        xs[width : 2 * width, i * chunk : (i + 1) * chunk] = lo

    contract = (((1,), (1,)), ((), ()))

    @pl.loop(0, levels // GROUP)
    def _(g):
        at = pl.ds(pl.multiple_of(g * GROUP, GROUP), GROUP)
        v = v_ref[0, at, :]
        his, los = [], []
        for i in range(2):
            b = (v[:, None, :] * ys[i][None]).reshape(GROUP * height, chunk)
            hi, lo = split(b)
            his.append(hi)
            los.append(lo)
        wide = lax.dot_general(
            jnp.concatenate(his, axis=1), xs[...], contract, preferred_element_type=jnp.float32
        )
        rest = lax.dot_general(
            jnp.concatenate(los, axis=1), xs[0:width, :], contract, preferred_element_type=jnp.float32
        )
        total = wide[:, :width] + wide[:, width:] + rest
        out_ref[at] += total.reshape(GROUP, height, width)

    @pl.when((t == pl.num_programs(0) - 1) & (c == pl.num_programs(1) - 1))
    def _():
        mask = mask_ref[...].astype(jnp.float32)

        @pl.loop(0, levels)
        def _(l):
            out_ref[l] = control_ref[l] + mask * out_ref[l]


def to_owner(values):
    return lax.all_to_all(
        lax.all_to_all(values, "lon", split_axis=2, concat_axis=2, tiled=True),
        "lat",
        split_axis=1,
        concat_axis=1,
        tiled=True,
    )


def shards(
    n_lon, n_lat, control, land_mask, std_dev, innovation, inverse_var,
    obs_row, obs_col, frac_row, frac_col, counts,
):
    levels = control.shape[0] * control.shape[1]
    height, width = control.shape[2:]
    slots = obs_row.shape[0] * obs_row.shape[1]
    chunk = min(CHUNK, slots)
    fields = control.reshape(levels, height, width)
    scales = std_dev.reshape(levels, 1)
    f32 = jnp.float32
    params = functools.partial(pltpu.CompilerParams, vmem_limit_bytes=VMEM_LIMIT)
    sems = pltpu.SemaphoreType.DMA((9,))

    meta = pl.pallas_call(
        meta_kernel,
        out_shape=jax.ShapeDtypeStruct((8, slots), f32),
        in_specs=[VMEM] * 6,
        out_specs=VMEM,
        compiler_params=params(),
        name="slot_weights",
    )(land_mask, obs_row, obs_col, frac_row, frac_col, counts)
    meta_all = pl.pallas_call(
        functools.partial(share_kernel, n_lon, n_lat),
        out_shape=jax.ShapeDtypeStruct((9, 8, slots), f32),
        in_specs=[VMEM],
        out_specs=VMEM,
        scratch_shapes=[sems, sems],
        compiler_params=params(collective_id=0, has_side_effects=True),
        name="share_slots",
    )(meta)

    owned = to_owner(jnp.concatenate([innovation, inverse_var], axis=0)).reshape(2 * levels, slots)

    grid = (9, slots // chunk)
    meta_spec = pl.BlockSpec((1, 8, chunk), lambda t, c: (t, 0, c))
    slot_spec = pl.BlockSpec((1, levels, chunk), lambda t, c: (t, 0, c))
    field_spec = pl.BlockSpec((levels, height, width), lambda t, c: (0, 0, 0))
    mask_spec = pl.BlockSpec((height, width), lambda t, c: (0, 0))
    parts = pl.pallas_call(
        forward_kernel,
        grid=grid,
        out_shape=jax.ShapeDtypeStruct((9, levels, slots), f32),
        in_specs=[meta_spec, field_spec, mask_spec],
        out_specs=slot_spec,
        scratch_shapes=[
            pltpu.VMEM((levels * height, 3 * width), jnp.bfloat16),
            pltpu.VMEM((2, height, chunk), f32),
            pltpu.VMEM((2, 3 * width, chunk), jnp.bfloat16),
        ],
        compiler_params=params(),
        name="partial_columns",
    )(meta_all, fields, land_mask)

    scaled = pl.pallas_call(
        functools.partial(misfit_kernel, n_lon, n_lat),
        out_shape=jax.ShapeDtypeStruct((9, levels, slots), f32),
        in_specs=[VMEM] * 4,
        out_specs=VMEM,
        scratch_shapes=[
            pltpu.VMEM((9, levels, slots), f32),
            pltpu.VMEM((levels, slots), f32),
            sems, sems, sems, sems,
        ],
        compiler_params=params(collective_id=1, has_side_effects=True),
        name="misfits",
    )(parts, owned, meta, scales)

    gradient = pl.pallas_call(
        backward_kernel,
        grid=grid,
        out_shape=jax.ShapeDtypeStruct((levels, height, width), f32),
        in_specs=[meta_spec, slot_spec, field_spec, mask_spec],
        out_specs=field_spec,
        scratch_shapes=[
            pltpu.VMEM((2, height, chunk), f32),
            pltpu.VMEM((2 * width, 2 * chunk), jnp.bfloat16),
        ],
        compiler_params=params(),
        name="gradient",
    )(meta_all, scaled, fields, land_mask)
    return gradient.reshape(control.shape)


def solution(mesh):
    tile = P("lat", "lon")
    in_specs = (
        P(None, None, "lat", "lon"), tile, P(),
        P(None, "lat", "lon"), P(None, "lat", "lon"),
        tile, tile, tile, tile, tile,
    )
    body = functools.partial(shards, mesh.shape["lon"], mesh.shape["lat"])
    return jax.shard_map(
        body, mesh=mesh, in_specs=in_specs,
        out_specs=P(None, None, "lat", "lon"), check_vma=False,
    )
```

time: 155 us -> 103 us (0.66)
  Pallas kernels: 0 us -> 83.2 us
  waiting for transfers between devices: 57.8 us -> 0.01 us
  local copies, waits for them, and re-layouts: 40.8 us -> 3.6 us
  starting transfers between devices: 24.3 us -> 4.72 us
  other arithmetic: 17.8 us -> 1.16 us
  matrix products: 12.4 us -> 0 us
  blocking collectives: 0 us -> 9.82 us
    pallas_call x0 -> x5, Pallas kernels: none -> 83.2 us  [the longest x1 31.7 us: shards(): pl.pallas_call(backward_kernel, grid=grid, out_shape=jax.ShapeDtypeStruct...]
    ppermute x8 -> x0, waiting for transfers between devices: 57.8 us -> none  [the longest x2 22.8 us: along_y(): lax.ppermute(field[:, height - HALF:], 'lat', [(i, i + 1) for i in range(...]
    ppermute x8 -> x0, starting transfers between devices: 13.7 us -> none  [the longest x2 6.37 us: along_y(): lax.ppermute(field[:, height - HALF:], 'lat', [(i, i + 1) for i in range(...]
    scatter-add x1 -> x0, other arithmetic: 13.6 us -> none  [shards(): jnp.zeros((rows_total, tile_rows * tile_cols), jnp.float32).at[:, index_all]]
    gather x8 -> x0, local copies, waits for them, and re-layouts: 13.3 us -> none  [shards(): columns = columns + weight[None] * jnp.take(table, corner + offset, axis=1)]
    dot_general x4 -> x0, matrix products: 12.4 us -> none  [the longest x2 7.64 us: along_x(): jnp.einsum('rye,xe->ryx', extended, band, precision=lax.Precision.HIGHEST)]
    all_to_all x0 -> x1, blocking collectives: none -> 9.82 us  [to_owner(): lax.all_to_all(values, 'lon', split_axis=2, concat_axis=2, tiled=True)]
    ppermute x8 -> x0, local copies, waits for them, and re-layouts: 9.65 us -> none  [the longest x2 4.32 us: padded_2(): lax.ppermute(head, axis, [((i + 1) % count, i) for i in range(count)])]
  transfers between devices with their start and end apart: 10 -> 1, of which waited for: 8 -> 0; matrix products, arithmetic and copies ran while one was open for 25% -> 0% of each run, Pallas kernels for 0% -> 36%
where the time goes in v2:
time: 103 us
  Pallas kernels  83.2 us (81%)
  blocking collectives  9.82 us (10%)
  starting transfers between devices  4.72 us (5%)
  local copies, waits for them, and re-layouts  3.6 us (3%)
  other arithmetic  1.16 us (1%)
    pallas_call x1, Pallas kernels, shards(): pl.pallas_call(backward_kernel, grid=grid, out_shape=jax.ShapeDtypeStruct...  31.7 us
    pallas_call x1, Pallas kernels, shards(): pl.pallas_call(forward_kernel, grid=grid, out_shape=jax.ShapeDtypeStruct(...  29.5 us
    pallas_call x1, Pallas kernels, shards(): pl.pallas_call(functools.partial(misfit_kernel, n_lon, n_lat), out_shape=...  14.7 us
    all_to_all x1, blocking collectives, to_owner(): lax.all_to_all(values, 'lon', split_axis=2, concat_axis=2, tiled=True)  9.82 us
    pallas_call x1, Pallas kernels, shards(): pl.pallas_call(functools.partial(share_kernel, n_lon, n_lat), out_shape=j...  7.08 us
    all_to_all x1, starting transfers between devices, to_owner(): lax.all_to_all(lax.all_to_all(values, 'lon', split_axis=2, concat_axis=2,...  4.72 us
    unnamed x22, local copies, waits for them, and re-layouts  2.22 us
  transfers between devices with their start and end apart: 1, of which 0 were waited for; matrix products, arithmetic and copies ran while one was open for 0% of the time, Pallas kernels for 36%

profile of v2, /device:TPU:1, one launch (start us, length us, event | category | flops | bytes accessed | tf_op | source)
XLA Modules:
  0.0 102.7 jit_solution(17810454821362937362)
XLA Ops:
  0.0 1.0 copy.23
  1.0 0.2 copy.24
  1.2 0.2 fusion
  1.4 0.0 copy-start
  1.4 0.2 reshape.17
  1.7 9.8 %all_to_all.10 = f32[8,1,4096]{2,1,0:T(1,128)S(1)} all-to-all(f32[8,1,4096]{2,1,0:T(1,128)S(1)} %reshape.17), channel_id=1, replica_groups=mesh['lon'=8,'lat'=4] {'lon'}, dimensions={0} | all-to-all | bytes 262144 | tf_op jit(solution)/shard_map/all_to_all | solution.py:279
  11.5 0.5 broadcast
  12.0 1.0 reduce
  12.9 0.2 reshape.18
  13.1 0.8 copy.25
  13.9 4.7 %all-to-all-start.1 = ((f32[64,4,128]{2,0,1:T(8,128)}), f32[64,4,128]{2,0,1:T(8,128)S(1)}, u32[]{:S(2)}, u32[]{:S(2)}) async-start(f32[64,4,128]{2,0,1:T(8,128)} %copy.25), calls=%async_computation.1 | async-start | bytes 262144 | tf_op jit(solution)/shard_map/all_to_all | solution.py:278
  18.6 0.0 copy-start.4
  18.7 0.0 copy-start.6
  18.7 0.1 reshape.16.std_ref
  18.8 0.5 copy-done.2
  19.3 0.0 copy-done.3
  19.3 0.0 copy-done.4
  19.3 0.0 copy-done.5
  19.4 0.0 copy-done.6
  19.4 0.2 slot_weights.1.meta_ref
  19.6 7.1 %share_slots.1.meta_ref = f32[9,8,512]{2,1,0:T(8,128)S(1)} custom-call(f32[8,512]{1,0:T(8,128)S(1)} %slot_weights.1.meta_ref), custom_call_target="tpu_custom_call" | custom-call | tf_op jit(solution)/shard_map/share_slots/pallas_call | solution.py:309
  26.7 29.5 %partial_columns.1.part_ref = f32[9,32,512]{2,1,0:T(8,128)S(1)} custom-call(f32[9,8,512]{2,1,0:T(8,128)S(1)} %share_slots.1.meta_ref, f32[32,64,128]{2,1,0:T(8,128)S(1)} %bitcast.10, s32[64,128]{1,0:T(8,128)S(1)} %copy-done.1), custom_call_target="tpu_custom_call" | custom-call | tf_op jit(solution)/shard_map/partial_columns/pallas_call | solution.py:326
  56.2 14.7 %misfits.1.v_ref = f32[9,32,512]{2,1,0:T(8,128)S(1)} custom-call(f32[9,32,512]{2,1,0:T(8,128)S(1)} %partial_columns.1.part_ref, f32[64,512]{1,0:T(8,128)S(1)} %copy_bitcast_fusion.owned_ref, f32[8,512]{1,0:T(8,128)S(1)} %slot_weights.1.meta_ref, f32[32,1]{1,0:T(8,128)S(1)} %reshape.16.std_ref), custom_call_target="tpu_custom_call" | custom-call | tf_op jit(solution)/shard_map/misfits/pallas_call | solution.py:341
  70.9 31.7 %gradient.1 = f32[32,64,128]{2,1,0:T(8,128)} custom-call(f32[9,8,512]{2,1,0:T(8,128)S(1)} %share_slots.1.meta_ref, f32[9,32,512]{2,1,0:T(8,128)S(1)} %misfits.1.v_ref, f32[32,64,128]{2,1,0:T(8,128)S(1)} %bitcast.11, s32[64,128]{1,0:T(8,128)S(1)} %copy-done.1), custom_call_target="tpu_custom_call" | custom-call | tf_op jit(solution)/shard_map/gradient/pallas_call | solution.py:355
  (12 shorter events, 0.0 us)
Async XLA Ops:
  0.0 1.0 copy-start.7
  1.4 25.3 %copy-start = (f32[2,16,64,128]{3,2,1,0:T(8,128)S(1)}, f32[2,16,64,128]{3,2,1,0:T(8,128)}, u32[]{:S(2)}) copy-start(f32[2,16,64,128]{3,2,1,0:T(8,128)} %param.10) | copy-start | bytes 3145732
  13.9 4.7 %copy-start.8 = (f32[2,16]{1,0:T(2,128)S(1)}, f32[2,16]{1,0:T(2,128)}, u32[]{:S(2)}) copy-start(f32[2,16]{1,0:T(2,128)} %param.12) | copy-start | bytes 388
  13.9 4.9 %copy-start.1 = (s32[64,128]{1,0:T(8,128)S(1)}, s32[64,128]{1,0:T(8,128)}, u32[]{:S(2)}) copy-start(s32[64,128]{1,0:T(8,128)} %mask_ref.5) | copy-start | bytes 98308
  13.9 42.3 %all-to-all-start.1 = ((f32[64,4,128]{2,0,1:T(8,128)}), f32[64,4,128]{2,0,1:T(8,128)S(1)}, u32[]{:S(2)}, u32[]{:S(2)}) async-start(f32[64,4,128]{2,0,1:T(8,128)} %copy.25), calls=%async_computation.1 | async-start | bytes 262144 | tf_op jit(solution)/shard_map/all_to_all | solution.py:278
  18.6 0.7 copy-start.2
  18.6 0.7 copy-start.3
  18.6 0.7 copy-start.4
  18.7 0.7 copy-start.5
  18.7 0.7 copy-start.6
